TPU v7x, 32 devices: a whole 2x2x4 slice. The times are simulated.
32 devices in a mesh: section: 4 (over x, core), dp: 4 (over z), sp: 2 (over y).
Axes of the slice: x: 2, y: 2, z: 4, core: 2. Of those that a mesh axis runs over, the one named last changes fastest.
Arguments:
- projected: bfloat16 [4, 4, 256, 3, 24, 128], P('section', 'dp', 'sp'), may hold values from -100 to 100, as said below
- seg_ids: int32 [4, 4, 256], P('section', 'dp'), may hold values from 0 to 7, never falling along the last dimension, each value on 1 to 64 neighbouring positions
- condition: bfloat16 [4, 32, 3072], P('section', 'dp'), may hold values from -8 to 8
- w_gate: bfloat16 [4, 3072, 3072], P('section', 'dp'), may hold values from -0.109375 to 0.109375
Outputs:
- handed: bfloat16 [4, 4, 256, 3072], P('section', 'dp', 'sp')
Inputs may be any that keep to these rules, and one draw needn't show every extreme that they name: `projected`: Query, key and value entries lie within the range. `seg_ids`: within a row the sample numbers never fall; each of the 8 samples holds 1 to 64 positions and one holds exactly 64.
All inputs are finite; a program needn't handle non-finite values.
Results may differ from a plain program's by a relative error of at most 0.006.
Values may be sent and summed in bfloat16 or wider, within the bound.
A program may use at most 64 MiB of HBM per device.

v0:
```python
import math

import jax
import jax.numpy as jnp
from jax import lax
from jax.sharding import PartitionSpec as P

masked_score = -1e30


def from_behind(block, axis, distance):
    devices = range(lax.axis_size(axis))
    route = [((i - distance) % len(devices), i) for i in devices]
    return lax.ppermute(block, axis, route)


def attend_row(exchanged, segment_row):
    query_rows = exchanged[:, 0]
    key_rows = exchanged[:, 1]
    values = exchanged[:, 2]
    length = query_rows.shape[0]
    query_block = min(512, length)
    block_count = length // query_block
    scale_factor = 1.0 / math.sqrt(query_rows.shape[2])

    def one_block(block_index):
        scores = (
            jnp.einsum("qhd,khd->hqk", query_rows, key_rows, preferred_element_type=jnp.float32)
            * scale_factor
        )
        same_segment = segment_row[:, None] == segment_row[None, :]
        scores = jnp.where(same_segment[None], scores, masked_score)
        row_max = jnp.max(scores, axis=2, keepdims=True)
        weights = jnp.exp(scores - row_max)
        row_total = jnp.sum(weights, axis=2, keepdims=True)
        rounded = weights.astype(jnp.bfloat16)
        mixed_out = jnp.einsum("hqk,khd->qhd", rounded, values, preferred_element_type=jnp.float32)
        mixed_out = mixed_out / jnp.transpose(row_total, (1, 0, 2))
        return mixed_out.astype(jnp.bfloat16)

    blocks = lax.map(one_block, jnp.arange(block_count, dtype=jnp.int32))
    return blocks.reshape(length, blocks.shape[2], blocks.shape[3])


def shards(projected, seg_ids, condition, w_gate):
    tok_rows = projected.shape[2]
    head_count = projected.shape[4]
    head_size = projected.shape[5]
    model_width = head_count * head_size
    group_count = lax.axis_size("sp")
    joined_rows = projected.reshape(tok_rows, 3, group_count, head_count // group_count, head_size)
    segment_row = seg_ids.reshape(-1)
    attended = attend_row(
        lax.all_to_all(joined_rows, "sp", split_axis=2, concat_axis=0, tiled=True)[:, :, 0],
        segment_row,
    )
    merged = lax.all_to_all(attended, "sp", split_axis=0, concat_axis=1, tiled=True).reshape(
        tok_rows, model_width
    )
    cond_act = jax.nn.silu(condition[0].astype(jnp.float32)).astype(jnp.bfloat16)
    rows_weight = w_gate[0]
    seg_count = cond_act.shape[0]
    slices = lax.all_to_all(cond_act, "dp", split_axis=1, concat_axis=0, tiled=True)
    seg_gate = lax.psum_scatter(
        jnp.dot(slices, rows_weight, preferred_element_type=jnp.float32),
        "dp",
        scatter_dimension=0,
        tiled=True,
    )
    local_segments = lax.dynamic_slice_in_dim(
        segment_row, lax.axis_index("sp") * tok_rows, tok_rows, 0
    )
    one_hot = (local_segments[:, None] == jnp.arange(seg_count, dtype=jnp.int32)[None, :]).astype(
        jnp.float32
    )
    token_gate = jnp.dot(one_hot, seg_gate, precision=lax.Precision.HIGHEST)
    gated_out = (token_gate * merged.astype(jnp.float32)).astype(jnp.bfloat16)
    handed = from_behind(gated_out, "section", 1)
    return handed.reshape(1, 1, tok_rows, model_width)


def solution(mesh):
    placed = (
        P("section", "dp", "sp", None, None, None),
        P("section", "dp", None),
        P("section", "dp", None),
        P("section", "dp", None),
    )
    return jax.shard_map(
        shards,
        mesh=mesh,
        in_specs=placed,
        out_specs=P("section", "dp", "sp", None),
        check_vma=False,
    )
```

profile of v0, /device:TPU:0, one launch (start us, length us, event | category | flops | bytes accessed | tf_op | source)
XLA Modules:
  0.0 92.2 jit_solution(11297740863175740281)
XLA Ops:
  6.5 1.5 %fusion.19 = bf16[8,4,768]{2,0,1:T(8,128)(2,1)} fusion(bf16[8,4,768]{2,0,1:T(8,128)(2,1)} %bitcast.54), kind=kLoop, calls=%fused_computation.27 | loop fusion | flops 147456 | bytes 98304 | tf_op jit(solution)/shard_map/convert_element_type | solution.py:60
  8.0 6.3 %all-to-all-start = ((bf16[8,4,768]{2,0,1:T(8,128)(2,1)}), bf16[8,4,768]{2,0,1:T(8,128)(2,1)S(1)}, u32[]{:S(2)}, u32[]{:S(2)}) async-start(bf16[8,4,768]{2,0,1:T(8,128)(2,1)} %fusion.19), calls=%async_computation | async-start | bytes 98304 | tf_op jit(solution)/shard_map/all_to_all | solution.py:63
  14.3 2.2 %copy.19 = bf16[1,1,128,3,24,128]{5,2,4,3,1,0:T(8,128)(2,1)S(1)} copy(bf16[1,1,128,3,24,128]{5,4,3,2,1,0:T(8,128)(2,1)} %param.4) | data formatting | bytes 4718592 | tf_op args[0]
  16.6 1.6 %copy.20 = bf16[128,3,2,12,128]{4,0,3,1,2:T(8,128)(2,1)} copy(bf16[128,3,2,12,128]{4,0,3,2,1:T(8,128)(2,1)S(1)} %bitcast.48) | data formatting | bytes 4718592 | tf_op jit(solution)/shard_map/reshape | solution.py:51
  18.1 0.0 copy-start
  18.1 1.9 %all-to-all-done = bf16[8,4,768]{2,0,1:T(8,128)(2,1)S(1)} async-done(((bf16[8,4,768]{2,0,1:T(8,128)(2,1)}), bf16[8,4,768]{2,0,1:T(8,128)(2,1)S(1)}, u32[]{:S(2)}, u32[]{:S(2)}) %all-to-all-start) | async-done | bytes 49184 | tf_op jit(solution)/shard_map/all_to_all | solution.py:63
  20.0 3.8 %all-to-all-start.1 = ((bf16[128,3,2,12,128]{4,0,3,1,2:T(8,128)(2,1)}), bf16[128,3,2,12,128]{4,0,3,1,2:T(8,128)(2,1)S(1)}, u32[]{:S(2)}, u32[]{:S(2)}) async-start(bf16[128,3,2,12,128]{4,0,3,1,2:T(8,128)(2,1)} %copy.20), calls=%async_computation.2 | async-start | bytes 4718592 | tf_op jit(solution)/shard_map/all_to_all | solution.py:54
  23.8 0.0 reduce-scatter.2.cloned.1.call-start
  23.9 0.0 copy-done
  23.9 0.1 broadcast_compare_fusion
  24.0 4.0 %fusion = f32[32,3072]{1,0:T(8,128)} fusion(bf16[1,768,3072]{2,1,0:T(8,128)(2,1)} %param.7, bf16[8,4,768]{2,0,1:T(8,128)(2,1)S(1)} %all-to-all-done), kind=kOutput, calls=%fused_computation | convolution fusion | flops 150994944 | bytes 5160960 | tf_op jit(solution)/shard_map/dot_general | solution.py:65
  28.0 0.0 reduce-scatter.2.cloned.1.call-update
  28.0 22.3 %all-to-all-done.1 = bf16[128,3,2,12,128]{4,0,3,1,2:T(8,128)(2,1)S(1)} async-done(((bf16[128,3,2,12,128]{4,0,3,1,2:T(8,128)(2,1)}), bf16[128,3,2,12,128]{4,0,3,1,2:T(8,128)(2,1)S(1)}, u32[]{:S(2)}, u32[]{:S(2)}) %all-to-all-start.1) | async-done | bytes 2359328 | tf_op jit(solution)/shard_map/all_to_all | solution.py:54
  50.3 0.2 copy.21
  50.5 0.6 fusion.3
  51.1 0.7 fusion.4
  51.8 1.5 %fusion.8 = bf16[256,12,128]{2,0,1:T(8,128)(2,1)S(1)} fusion(f32[12,256,256]{1,2,0:T(8,128)S(1)} %get-tuple-element.16, f32[12,256]{1,0:T(8,128)S(1)} %get-tuple-element.15, pred[256,256]{0,1:T(8,128)(4,1)S(1)} %broadcast_compare_fusion, bf16[256,3,12,128]{3,0,2,1:T(8,128)(2,1)S(1)} %bitcast.52, f32[256,12]{0,1:T(8,128)S(1)} %bitcast.55), kind=kOutput, calls=%fused_computation.12 | convolution fusion | flops 205258752 | bytes 4816896 | tf_op jit(solution)/shard_map/while/body/eval_jaxpr/hqk,khd->qhd/dot_general | solution.py:37
  53.2 1.5 %copy.23 = bf16[256,12,128]{2,1,0:T(8,128)(2,1)} copy(bf16[256,12,128]{2,0,1:T(8,128)(2,1)S(1)} %fusion.8) | data formatting | bytes 1572864 | tf_op jit(solution)/shard_map/while/body/eval_jaxpr/convert_element_type | solution.py:39
  54.7 3.6 %all-to-all-start.2 = ((bf16[256,12,128]{2,1,0:T(8,128)(2,1)}), bf16[256,12,128]{2,1,0:T(8,128)(2,1)S(1)}, u32[]{:S(2)}, u32[]{:S(2)}) async-start(bf16[256,12,128]{2,1,0:T(8,128)(2,1)} %copy.23), calls=%async_computation.3 | async-start | bytes 2097152 | tf_op jit(solution)/shard_map/all_to_all | solution.py:57
  58.3 11.6 %all-to-all-done.2 = bf16[256,12,128]{2,1,0:T(8,128)(2,1)S(1)} async-done(((bf16[256,12,128]{2,1,0:T(8,128)(2,1)}), bf16[256,12,128]{2,1,0:T(8,128)(2,1)S(1)}, u32[]{:S(2)}, u32[]{:S(2)}) %all-to-all-start.2) | async-done | bytes 786464 | tf_op jit(solution)/shard_map/all_to_all | solution.py:57
  69.9 0.2 copy.24
  70.1 0.2 convert_bitcast_fusion
  70.3 0.5 copy.25
  70.8 0.5 copy.26
  71.3 0.0 reduce-scatter.2.cloned.1.call-done
  71.3 1.7 %fusion.2 = bf16[128,3072]{1,0:T(8,128)(2,1)S(1)} fusion(f32[128,3072]{1,0:T(8,128)S(1)} %copy.26, f32[8,3072]{1,0:T(8,128)} %reduce-scatter.2.cloned.1.call-done, s32[128]{0:T(128)S(1)} %dynamic-slice_bitcast_fusion), kind=kOutput, calls=%fused_computation.3 | convolution fusion | flops 38536192 | bytes 2458112 | tf_op jit(solution)/shard_map/dot_general | solution.py:76
  73.0 0.1 collective-permute-start
  73.1 11.4 %collective-permute-done = bf16[128,3072]{1,0:T(8,128)(2,1)S(1)} collective-permute-done((bf16[128,3072]{1,0:T(8,128)(2,1)S(1)}, bf16[128,3072]{1,0:T(8,128)(2,1)S(1)}, u32[]{:S(2)}, u32[]{:S(2)}) %collective-permute-start) | collective-permute-done | bytes 786464 | tf_op jit(solution)/shard_map/ppermute | solution.py:14
  84.5 0.9 copy.29
  (1 shorter events, 0.0 us)
Async XLA Ops:
  8.0 12.0 %all-to-all-start = ((bf16[8,4,768]{2,0,1:T(8,128)(2,1)}), bf16[8,4,768]{2,0,1:T(8,128)(2,1)S(1)}, u32[]{:S(2)}, u32[]{:S(2)}) async-start(bf16[8,4,768]{2,0,1:T(8,128)(2,1)} %fusion.19), calls=%async_computation | async-start | bytes 98304 | tf_op jit(solution)/shard_map/all_to_all | solution.py:63
  18.1 5.7 %copy-start = (s32[1,1,256]{2,1,0:T(1,128)S(1)}, s32[1,1,256]{2,1,0:T(1,128)}, u32[]{:S(2)}) copy-start(s32[1,1,256]{2,1,0:T(1,128)} %param.5) | copy-start | bytes 3076
  20.0 30.3 %all-to-all-start.1 = ((bf16[128,3,2,12,128]{4,0,3,1,2:T(8,128)(2,1)}), bf16[128,3,2,12,128]{4,0,3,1,2:T(8,128)(2,1)S(1)}, u32[]{:S(2)}, u32[]{:S(2)}) async-start(bf16[128,3,2,12,128]{4,0,3,1,2:T(8,128)(2,1)} %copy.20), calls=%async_computation.2 | async-start | bytes 4718592 | tf_op jit(solution)/shard_map/all_to_all | solution.py:54
  23.8 47.5 %reduce-scatter.2.cloned.1.call-start = ((), (), s32[]{:S(2)}) async-start(), calls=%async_computation.4 | async-start | bytes 491520 | tf_op jit(solution)/shard_map/reduce_scatter | solution.py:64
  54.7 15.2 %all-to-all-start.2 = ((bf16[256,12,128]{2,1,0:T(8,128)(2,1)}), bf16[256,12,128]{2,1,0:T(8,128)(2,1)S(1)}, u32[]{:S(2)}, u32[]{:S(2)}) async-start(bf16[256,12,128]{2,1,0:T(8,128)(2,1)} %copy.23), calls=%async_computation.3 | async-start | bytes 2097152 | tf_op jit(solution)/shard_map/all_to_all | solution.py:57
  73.0 11.5 %collective-permute-start = (bf16[128,3072]{1,0:T(8,128)(2,1)S(1)}, bf16[128,3072]{1,0:T(8,128)(2,1)S(1)}, u32[]{:S(2)}, u32[]{:S(2)}) collective-permute-start(bf16[128,3072]{1,0:T(8,128)(2,1)S(1)} %fusion.2), channel_id=1, source_target_pairs={{24,0},{0,8},{8,16},{16,24},{25,1},{1,9},{9,17},{17,25},{26,2},{2,... | collective-permute-start | bytes 2359304 | tf_op jit(solution)/shard_map/ppermute | solution.py:14
Sparse Core Ops, SparseCore 0:
  28.1 20.7 reduce-scatter.1
where the time goes:
time: 92.7 us; the launch traced here: 92.2 us
  waiting for transfers between devices  47.2 us (51%)
  starting transfers between devices  13.8 us (15%)
  between operations  13.5 us (15%)
  matrix products  7.8 us (8%)
  local copies, waits for them, and re-layouts  7.53 us (8%)
  other arithmetic  2.39 us (3%)
    all_to_all x1, waiting for transfers between devices, shards(): lax.all_to_all(joined_rows, 'sp', split_axis=2, concat_axis=0, tiled=True)  22.3 us
    all_to_all x1, waiting for transfers between devices, shards(): lax.all_to_all(attended, 'sp', split_axis=0, concat_axis=1, tiled=True)  11.6 us
    ppermute x1, waiting for transfers between devices, from_behind(): return lax.ppermute(block, axis, route)  11.4 us
    all_to_all x1, starting transfers between devices, shards(): lax.all_to_all(cond_act, 'dp', split_axis=1, concat_axis=0, tiled=True)  6.32 us
    dot_general x1, matrix products, shards(): jnp.dot(slices, rows_weight, preferred_element_type=jnp.float32)  4 us
    all_to_all x1, starting transfers between devices, shards(): lax.all_to_all(joined_rows, 'sp', split_axis=2, concat_axis=0, tiled=True)  3.81 us
    all_to_all x1, starting transfers between devices, shards(): lax.all_to_all(attended, 'sp', split_axis=0, concat_axis=1, tiled=True)  3.58 us
    unnamed x4, local copies, waits for them, and re-layouts  3.13 us
  transfers between devices with their start and end apart: 5, of which 4 were waited for; matrix products, arithmetic and copies ran while one was open for 15% of the time, Pallas kernels for 0%

commit v1 on v0

v1 whole, which is shorter than its diff:
```python
import functools
import math

import jax
import jax.numpy as jnp
from jax import lax
from jax.experimental import pallas as pl
from jax.experimental.pallas import tpu as pltpu
from jax.sharding import PartitionSpec as P

masked_score = -1e30
HEADS_PER_CHUNK = 2
CHUNKS_BEFORE_GATE = 4
GATE_TILE = 512
MESH = pl.DeviceIdType.MESH


def relay_kernel(
    sizes,
    x_hbm,
    seg_ref,
    cond_ref,
    w_hbm,
    out_hbm,
    x_vmem,
    w_vmem,
    k_halo,
    v_halo,
    stage,
    act_own,
    act_all,
    partial,
    gate_parts,
    gate_split,
    bias,
    x_sem,
    w_sem,
    k_send,
    k_recv,
    v_send,
    v_recv,
    act_send,
    act_recv,
    part_send,
    part_recv,
    out_send,
    out_recv,
):
    tok, heads, size, length, samples, n_section, n_dp, n_sp, reach = sizes
    width = heads * size
    w_rows = w_vmem.shape[0]
    chunk = HEADS_PER_CHUNK * size
    chunks = heads // HEADS_PER_CHUNK
    section, dp, sp = lax.axis_index("section"), lax.axis_index("dp"), lax.axis_index("sp")
    after = lax.rem(section + 1, n_section)
    before = lax.rem(section + n_section - 1, n_section)

    if n_sp == 1:
        exchanges = []
    elif n_sp == 2:
        exchanges = [(1 - sp, (1 - sp) * (tok - reach), 1 - sp, sp * (tok - reach))]
    else:
        right, left = lax.rem(sp + 1, n_sp), lax.rem(sp + n_sp - 1, n_sp)
        exchanges = [(right, tok - reach, left, tok - reach), (left, 0, right, 0)]
    slots = len(exchanges)

    x_copy = pltpu.make_async_copy(x_hbm, x_vmem, x_sem)
    w_copy = pltpu.make_async_copy(w_hbm.at[0], w_vmem, w_sem)
    x_copy.start()
    w_copy.start()

    barrier = pltpu.get_barrier_semaphore()
    for peer, _, _, _ in exchanges:
        pl.semaphore_signal(barrier, inc=1, device_id=(section, dp, peer), device_id_type=MESH)

    def greet(d, carry):
        pl.semaphore_signal(
            barrier, inc=1, device_id=(section, lax.rem(dp + d, n_dp), sp), device_id_type=MESH
        )
        return carry

    lax.fori_loop(1, n_dp, greet, 0)
    for peer in (after, before):
        pl.semaphore_signal(barrier, inc=1, device_id=(peer, dp, sp), device_id_type=MESH)

    cond = cond_ref[0].astype(jnp.float32)
    act = (cond / (1.0 + jnp.exp(-cond))).astype(jnp.bfloat16).astype(jnp.float32)
    for j in range(n_dp):
        act_own[j] = act[:, j * w_rows : (j + 1) * w_rows]

    pl.semaphore_wait(barrier, slots + n_dp - 1 + 2)

    def act_copy(d):
        peer = lax.rem(dp + d, n_dp)
        return pltpu.make_async_remote_copy(
            src_ref=act_own.at[peer],
            dst_ref=act_all.at[dp],
            send_sem=act_send.at[d],
            recv_sem=act_recv.at[d],
            device_id=(section, peer, sp),
            device_id_type=MESH,
        )

    def halo_copies(slot, c):
        peer, row, _, _ = exchanges[slot]
        rows = pl.ds(row if isinstance(row, int) else pl.multiple_of(row, reach), reach)
        lanes = pl.multiple_of(c * chunk, chunk)
        result = []
        for part, held, send, recv in ((1, k_halo, k_send, k_recv), (2, v_halo, v_send, v_recv)):
            result.append(
                pltpu.make_async_remote_copy(
                    src_ref=x_hbm.at[rows, pl.ds(part * width + lanes, chunk)],
                    dst_ref=held.at[slot, rows, pl.ds(lanes, chunk)],
                    send_sem=send.at[slot, c],
                    recv_sem=recv.at[slot, c],
                    device_id=(section, dp, peer),
                    device_id_type=MESH,
                )
            )
        return result

    def arrived_copies(slot, c):
        _, _, _, row = exchanges[slot]
        rows = pl.ds(row if isinstance(row, int) else pl.multiple_of(row, reach), reach)
        lanes = pl.multiple_of(c * chunk, chunk)
        result = []
        for part, held, send, recv in ((1, k_halo, k_send, k_recv), (2, v_halo, v_send, v_recv)):
            result.append(
                pltpu.make_async_remote_copy(
                    src_ref=x_hbm.at[rows, pl.ds(part * width + lanes, chunk)],
                    dst_ref=held.at[slot, rows, pl.ds(lanes, chunk)],
                    send_sem=send.at[slot, c],
                    recv_sem=recv.at[slot, c],
                    device_id=(section, dp, exchanges[slot][0]),
                    device_id_type=MESH,
                )
            )
        return result

    def part_copy(d):
        peer = lax.rem(dp + d, n_dp)
        return pltpu.make_async_remote_copy(
            src_ref=partial.at[peer],
            dst_ref=gate_parts.at[d],
            send_sem=part_send.at[d],
            recv_sem=part_recv.at[d],
            device_id=(section, peer, sp),
            device_id_type=MESH,
        )

    def out_copy(c):
        lanes = pl.ds(pl.multiple_of(c * chunk, chunk), chunk)
        return pltpu.make_async_remote_copy(
            src_ref=stage.at[:, lanes],
            dst_ref=out_hbm.at[:, lanes],
            send_sem=out_send.at[c],
            recv_sem=out_recv.at[c],
            device_id=(after, dp, sp),
            device_id_type=MESH,
        )

    def start_act(d, carry):
        act_copy(d).start()
        return carry

    lax.fori_loop(1, n_dp, start_act, 0)

    def start_halo(c, carry):
        for slot in range(slots):
            for copy in halo_copies(slot, c):
                copy.start()
        return carry

    lax.fori_loop(0, chunks, start_halo, 0)

    if slots and reach < tok:
        for slot in range(slots):
            row = exchanges[slot][3]
            empty = tok - reach
            first = (reach if row == 0 else 0) if isinstance(row, int) else (1 - sp) * reach
            rows = pl.ds(first if isinstance(first, int) else pl.multiple_of(first, empty), empty)
            k_halo[slot, rows, :] = jnp.zeros((empty, width), jnp.bfloat16)
            v_halo[slot, rows, :] = jnp.zeros((empty, width), jnp.bfloat16)

    def block_segments(index):
        found = jnp.zeros((1, tok), jnp.float32)
        for b in range(n_sp):
            ids = seg_ref[0, :, b * tok : (b + 1) * tok].astype(jnp.float32)
            found = found + jnp.where(index == b, ids, 0.0)
        return found

    own_segments = block_segments(sp)
    query_segments = jnp.transpose(jnp.broadcast_to(own_segments, (tok, tok)))
    for slot in range(slots + 1):
        ids = own_segments if slot == 0 else block_segments(exchanges[slot - 1][2])
        bias[:, slot * tok : (slot + 1) * tok] = jnp.where(
            query_segments == ids, 0.0, masked_score
        )
    which = lax.broadcasted_iota(jnp.int32, (tok, 2 * samples), 1)
    which = jnp.where(which >= samples, which - samples, which).astype(jnp.float32)
    chosen = jnp.where(query_segments[:, : 2 * samples] == which, 1.0, 0.0).astype(jnp.bfloat16)

    act_all[dp] = act_own[dp]

    def wait_act(d, carry):
        act_copy(d).wait_recv()
        return carry

    lax.fori_loop(1, n_dp, wait_act, 0)
    w_copy.wait()
    act_rows = act_all[...].reshape(n_dp * samples, w_rows).astype(jnp.bfloat16)

    def gate_tile(t, carry):
        lanes = pl.ds(pl.multiple_of(t * GATE_TILE, GATE_TILE), GATE_TILE)
        sums = jnp.dot(act_rows, w_vmem[:, lanes], preferred_element_type=jnp.float32)
        partial[:, :, lanes] = sums.reshape(n_dp, samples, GATE_TILE)
        return carry

    lax.fori_loop(0, width // GATE_TILE, gate_tile, 0)

    def start_part(d, carry):
        part_copy(d).start()
        return carry

    lax.fori_loop(1, n_dp, start_part, 0)

    x_copy.wait()
    factor = math.log2(math.e) / math.sqrt(size)
    contract_last = (((1,), (1,)), ((), ()))

    def attend(c):
        for slot in range(slots):
            for copy in arrived_copies(slot, c):
                copy.wait_recv()
        base = pl.multiple_of(c * chunk, chunk)
        for h in range(HEADS_PER_CHUNK):
            lane = base + h * size
            lanes = pl.ds(lane, size)
            query = x_vmem[:, lanes]
            keys = [x_vmem[:, pl.ds(width + lane, size)]]
            values = [x_vmem[:, pl.ds(2 * width + lane, size)]]
            for slot in range(slots):
                keys.append(k_halo[slot, :, lanes])
                values.append(v_halo[slot, :, lanes])
            scores = [
                lax.dot_general(query, key, contract_last, preferred_element_type=jnp.float32)
                + bias[:, i * tok : (i + 1) * tok]
                for i, key in enumerate(keys)
            ]
            top = functools.reduce(jnp.maximum, scores)
            top = jnp.max(top, axis=1, keepdims=True)
            weights = [jnp.exp2((s - top) * factor) for s in scores]
            total = jnp.sum(functools.reduce(jnp.add, weights), axis=1, keepdims=True)
            mixed = sum(
                jnp.dot(w.astype(jnp.bfloat16), v, preferred_element_type=jnp.float32)
                for w, v in zip(weights, values)
            )
            stage[:, lanes] = (mixed / total).astype(jnp.bfloat16)

    def gate_and_send(c):
        lanes = pl.ds(pl.multiple_of(c * chunk, chunk), chunk)
        token_gate = jnp.dot(chosen, gate_split[:, lanes], preferred_element_type=jnp.float32)
        stage[:, lanes] = (token_gate * stage[:, lanes].astype(jnp.float32)).astype(jnp.bfloat16)
        out_copy(c).start()

    def early(c, carry):
        attend(c)
        return carry

    def late(c, carry):
        attend(c)
        gate_and_send(c)
        return carry

    def only_send(c, carry):
        gate_and_send(c)
        return carry

    lax.fori_loop(0, CHUNKS_BEFORE_GATE, early, 0)

    gate_parts[0] = partial[dp]

    def add_part(d, total):
        part_copy(d).wait_recv()
        return total + gate_parts[d]

    gate = lax.fori_loop(1, n_dp, add_part, gate_parts[0])
    high = gate.astype(jnp.bfloat16).astype(jnp.float32)
    gate_split[...] = jnp.concatenate([high, gate - high], axis=0).astype(jnp.bfloat16)

    lax.fori_loop(0, CHUNKS_BEFORE_GATE, only_send, 0)
    lax.fori_loop(CHUNKS_BEFORE_GATE, chunks, late, 0)

    def finish_small(d, carry):
        act_copy(d).wait_send()
        part_copy(d).wait_send()
        return carry

    lax.fori_loop(1, n_dp, finish_small, 0)

    def finish(c, carry):
        for slot in range(slots):
            for copy in halo_copies(slot, c):
                copy.wait_send()
        out_copy(c).wait()
        return carry

    lax.fori_loop(0, chunks, finish, 0)


def shards(projected, seg_ids, condition, w_gate):
    tok, heads, size = projected.shape[2], projected.shape[4], projected.shape[5]
    width = heads * size
    length = seg_ids.shape[2]
    samples, w_rows = condition.shape[1], w_gate.shape[1]
    n_section, n_dp, n_sp = (lax.axis_size(a) for a in ("section", "dp", "sp"))
    reach = min(tok, length // 4)
    slots = 0 if n_sp == 1 else 1 if n_sp == 2 else 2
    chunks = heads // HEADS_PER_CHUNK
    sizes = (tok, heads, size, length, samples, n_section, n_dp, n_sp, reach)
    anywhere = pl.BlockSpec(memory_space=pl.ANY)
    inside = pl.BlockSpec(memory_space=pltpu.VMEM)
    dma = pltpu.SemaphoreType.DMA
    keys = (slots + 1) * tok
    handed = pl.pallas_call(
        functools.partial(relay_kernel, sizes),
        out_shape=jax.ShapeDtypeStruct((tok, width), jnp.bfloat16),
        in_specs=[anywhere, inside, inside, anywhere],
        out_specs=anywhere,
        scratch_shapes=[
            pltpu.VMEM((tok, 3 * width), jnp.bfloat16),
            pltpu.VMEM((w_rows, width), jnp.bfloat16),
            pltpu.VMEM((max(slots, 1), tok, width), jnp.bfloat16),
            pltpu.VMEM((max(slots, 1), tok, width), jnp.bfloat16),
            pltpu.VMEM((tok, width), jnp.bfloat16),
            pltpu.VMEM((n_dp, samples, w_rows), jnp.float32),
            pltpu.VMEM((n_dp, samples, w_rows), jnp.float32),
            pltpu.VMEM((n_dp, samples, width), jnp.float32),
            pltpu.VMEM((n_dp, samples, width), jnp.float32),
            pltpu.VMEM((2 * samples, width), jnp.bfloat16),
            pltpu.VMEM((tok, keys), jnp.float32),
            dma,
            dma,
            dma((max(slots, 1), chunks)),
            dma((max(slots, 1), chunks)),
            dma((max(slots, 1), chunks)),
            dma((max(slots, 1), chunks)),
            dma((n_dp,)),
            dma((n_dp,)),
            dma((n_dp,)),
            dma((n_dp,)),
            dma((chunks,)),
            dma((chunks,)),
        ],
        compiler_params=pltpu.CompilerParams(
            collective_id=0, has_side_effects=True, vmem_limit_bytes=60 * 1024 * 1024
        ),
        cost_estimate=pl.CostEstimate(
            flops=4 * tok * keys * width + 2 * n_dp * samples * w_rows * width,
            bytes_accessed=2 * (3 * tok * width + w_rows * width + tok * width),
            transcendentals=tok * keys * heads,
        ),
    )(projected.reshape(tok, 3 * width), seg_ids, condition, w_gate)
    return handed.reshape(1, 1, tok, width)


def solution(mesh):
    placed = (
        P("section", "dp", "sp", None, None, None),
        P("section", "dp", None),
        P("section", "dp", None),
        P("section", "dp", None),
    )
    return jax.shard_map(
        shards,
        mesh=mesh,
        in_specs=placed,
        out_specs=P("section", "dp", "sp", None),
        check_vma=False,
    )
```

time: 92.7 us -> 36.4 us (0.39)
  the two profiles are of different devices: /device:TPU:0 before, /device:TPU:14 now
where the time goes in v1:
time: 36.4 us; the launch traced here: 36.1 us
  Pallas kernels  29.7 us (82%)
  local copies, waits for them, and re-layouts  6.37 us (18%)
    pallas_call x1, Pallas kernels, shards(): pl.pallas_call(functools.partial(relay_kernel, sizes), out_shape=jax.Shap...  29.7 us
    reshape x1, local copies, waits for them, and re-layouts, shards(): projected.reshape(tok, 3 * width)  4.31 us
    unnamed x1, local copies, waits for them, and re-layouts  2.06 us

profile of v1, /device:TPU:14, one launch (start us, length us, event | category | flops | bytes accessed | tf_op | source)
XLA Modules:
  0.0 36.1 jit_solution(7434587080037614291)
XLA Ops:
  0.0 4.3 %reshape.6.x_hbm = bf16[128,9216]{1,0:T(8,128)(2,1)} reshape(bf16[1,1,128,3,24,128]{5,4,3,2,1,0:T(8,128)(2,1)} %param.4) | data formatting | bytes 4718592 | tf_op jit(solution)/shard_map/reshape | solution.py:363
  4.3 29.7 %shard_map.46 = bf16[128,3072]{1,0:T(8,128)(2,1)} custom-call(bf16[128,9216]{1,0:T(8,128)(2,1)} %reshape.6.x_hbm, s32[1,1,256]{2,1,0:T(1,128)} %seg_ref.1, bf16[1,8,3072]{2,1,0:T(8,128)(2,1)} %cond_ref.1, bf16[1,768,3072]{2,1,0:T(8,128)(2,1)} %w_hbm.1), custom_call_target="tpu_custom_call" | custom-call | flops 553648128 | bytes 7864320 | tf_op jit(solution)/shard_map/pallas_call | solution.py:325
  34.0 2.1 %copy.6 = bf16[1,1,128,3072]{3,2,1,0:T(8,128)(2,1)} copy(bf16[1,1,128,3072]{3,2,1,0:T(8,128)(2,1)} %bitcast.3) | data formatting | bytes 1572864

commit v2 on v1

--- a/solution.py
+++ b/solution.py
@@ -10,8 +10,8 @@
 
 masked_score = -1e30
 HEADS_PER_CHUNK = 2
-CHUNKS_BEFORE_GATE = 4
-GATE_TILE = 512
+CHUNKS_PER_TILE = 2
+TILES_BEFORE_GATE = 1
 MESH = pl.DeviceIdType.MESH
 
 
@@ -51,6 +51,8 @@
     w_rows = w_vmem.shape[0]
     chunk = HEADS_PER_CHUNK * size
     chunks = heads // HEADS_PER_CHUNK
+    tile = chunk * CHUNKS_PER_TILE
+    tiles = chunks // CHUNKS_PER_TILE
     section, dp, sp = lax.axis_index("section"), lax.axis_index("dp"), lax.axis_index("sp")
     after = lax.rem(section + 1, n_section)
     before = lax.rem(section + n_section - 1, n_section)
@@ -137,13 +139,14 @@
             )
         return result
 
-    def part_copy(d):
+    def part_copy(t, d):
         peer = lax.rem(dp + d, n_dp)
+        lanes = pl.ds(pl.multiple_of(t * tile, tile), tile)
         return pltpu.make_async_remote_copy(
-            src_ref=partial.at[peer],
-            dst_ref=gate_parts.at[d],
-            send_sem=part_send.at[d],
-            recv_sem=part_recv.at[d],
+            src_ref=partial.at[peer, :, lanes],
+            dst_ref=gate_parts.at[d, :, lanes],
+            send_sem=part_send.at[t, d],
+            recv_sem=part_recv.at[t, d],
             device_id=(section, peer, sp),
             device_id_type=MESH,
         )
@@ -211,18 +214,18 @@
     act_rows = act_all[...].reshape(n_dp * samples, w_rows).astype(jnp.bfloat16)
 
     def gate_tile(t, carry):
-        lanes = pl.ds(pl.multiple_of(t * GATE_TILE, GATE_TILE), GATE_TILE)
+        lanes = pl.ds(pl.multiple_of(t * tile, tile), tile)
         sums = jnp.dot(act_rows, w_vmem[:, lanes], preferred_element_type=jnp.float32)
-        partial[:, :, lanes] = sums.reshape(n_dp, samples, GATE_TILE)
-        return carry
-
-    lax.fori_loop(0, width // GATE_TILE, gate_tile, 0)
-
-    def start_part(d, carry):
-        part_copy(d).start()
-        return carry
-
-    lax.fori_loop(1, n_dp, start_part, 0)
+        partial[:, :, lanes] = sums.reshape(n_dp, samples, tile)
+
+        def start_part(d, carry):
+            part_copy(t, d).start()
+            return carry
+
+        lax.fori_loop(1, n_dp, start_part, 0)
+        return carry
+
+    lax.fori_loop(0, tiles, gate_tile, 0)
 
     x_copy.wait()
     factor = math.log2(math.e) / math.sqrt(size)
@@ -263,37 +266,46 @@
         stage[:, lanes] = (token_gate * stage[:, lanes].astype(jnp.float32)).astype(jnp.bfloat16)
         out_copy(c).start()
 
+    def sum_gate(t):
+        lanes = pl.ds(pl.multiple_of(t * tile, tile), tile)
+
+        def add_part(d, total):
+            part_copy(t, d).wait_recv()
+            return total + gate_parts[d, :, lanes]
+
+        gate = lax.fori_loop(1, n_dp, add_part, partial[dp, :, lanes])
+        high = gate.astype(jnp.bfloat16).astype(jnp.float32)
+        gate_split[:, lanes] = jnp.concatenate([high, gate - high], axis=0).astype(jnp.bfloat16)
+
     def early(c, carry):
         attend(c)
         return carry
 
-    def late(c, carry):
-        attend(c)
-        gate_and_send(c)
-        return carry
-
-    def only_send(c, carry):
-        gate_and_send(c)
-        return carry
-
-    lax.fori_loop(0, CHUNKS_BEFORE_GATE, early, 0)
-
-    gate_parts[0] = partial[dp]
-
-    def add_part(d, total):
-        part_copy(d).wait_recv()
-        return total + gate_parts[d]
-
-    gate = lax.fori_loop(1, n_dp, add_part, gate_parts[0])
-    high = gate.astype(jnp.bfloat16).astype(jnp.float32)
-    gate_split[...] = jnp.concatenate([high, gate - high], axis=0).astype(jnp.bfloat16)
-
-    lax.fori_loop(0, CHUNKS_BEFORE_GATE, only_send, 0)
-    lax.fori_loop(CHUNKS_BEFORE_GATE, chunks, late, 0)
+    def only_send(t, carry):
+        sum_gate(t)
+        for i in range(CHUNKS_PER_TILE):
+            gate_and_send(t * CHUNKS_PER_TILE + i)
+        return carry
+
+    def late(t, carry):
+        sum_gate(t)
+        for i in range(CHUNKS_PER_TILE):
+            attend(t * CHUNKS_PER_TILE + i)
+            gate_and_send(t * CHUNKS_PER_TILE + i)
+        return carry
+
+    lax.fori_loop(0, TILES_BEFORE_GATE * CHUNKS_PER_TILE, early, 0)
+    lax.fori_loop(0, TILES_BEFORE_GATE, only_send, 0)
+    lax.fori_loop(TILES_BEFORE_GATE, tiles, late, 0)
 
     def finish_small(d, carry):
         act_copy(d).wait_send()
-        part_copy(d).wait_send()
+
+        def finish_part(t, carry):
+            part_copy(t, d).wait_send()
+            return carry
+
+        lax.fori_loop(0, tiles, finish_part, 0)
         return carry
 
     lax.fori_loop(1, n_dp, finish_small, 0)
@@ -325,7 +337,7 @@
     handed = pl.pallas_call(
         functools.partial(relay_kernel, sizes),
         out_shape=jax.ShapeDtypeStruct((tok, width), jnp.bfloat16),
-        in_specs=[anywhere, inside, inside, anywhere],
+        in_specs=[anywhere, inside, inside, pl.BlockSpec(memory_space=pltpu.HBM)],
         out_specs=anywhere,
         scratch_shapes=[
             pltpu.VMEM((tok, 3 * width), jnp.bfloat16),
@@ -347,13 +359,13 @@
             dma((max(slots, 1), chunks)),
             dma((n_dp,)),
             dma((n_dp,)),
-            dma((n_dp,)),
-            dma((n_dp,)),
+            dma((chunks // CHUNKS_PER_TILE, n_dp)),
+            dma((chunks // CHUNKS_PER_TILE, n_dp)),
             dma((chunks,)),
             dma((chunks,)),
         ],
         compiler_params=pltpu.CompilerParams(
-            collective_id=0, has_side_effects=True, vmem_limit_bytes=60 * 1024 * 1024
+            collective_id=0, has_side_effects=True, vmem_limit_bytes=40 * 1024 * 1024
         ),
         cost_estimate=pl.CostEstimate(
             flops=4 * tok * keys * width + 2 * n_dp * samples * w_rows * width,

time: 36.4 us -> 34.6 us (0.951)
  the two profiles are of different devices: /device:TPU:14 before, /device:TPU:0 now
where the time goes in v2:
time: 34.6 us; the launch traced here: 34.4 us
  Pallas kernels  28.2 us (82%)
  local copies, waits for them, and re-layouts  6.18 us (18%)
    pallas_call x1, Pallas kernels, shards(): pl.pallas_call(functools.partial(relay_kernel, sizes), out_shape=jax.Shap...  28.2 us
    unnamed x7, local copies, waits for them, and re-layouts  3.22 us
    reshape x1, local copies, waits for them, and re-layouts, shards(): projected.reshape(tok, 3 * width)  2.96 us

profile of v2, /device:TPU:0, one launch (start us, length us, event | category | flops | bytes accessed | tf_op | source)
XLA Modules:
  0.0 34.4 jit_solution(1995335257073535556)
XLA Ops:
  0.0 0.0 copy-start.1
  0.0 0.0 copy-start.2
  0.0 3.0 %reshape.6.x_hbm = bf16[128,9216]{1,0:T(8,128)(2,1)S(1)} reshape(bf16[1,1,128,3,24,128]{5,4,3,2,1,0:T(8,128)(2,1)} %param.4) | data formatting | bytes 4718592 | tf_op jit(solution)/shard_map/reshape | solution.py:375
  3.0 0.0 copy-done.1
  3.0 0.0 copy-done.2
  3.0 0.0 copy-start
  3.0 2.3 %copy-done = bf16[1,768,3072]{2,1,0:T(8,128)(2,1)S(1)} copy-done((bf16[1,768,3072]{2,1,0:T(8,128)(2,1)S(1)}, bf16[1,768,3072]{2,1,0:T(8,128)(2,1)}, u32[]{:S(2)}) %copy-start) | copy-done | bytes 4718616
  5.3 28.2 %shard_map.46 = bf16[128,3072]{1,0:T(8,128)(2,1)S(1)} custom-call(bf16[128,9216]{1,0:T(8,128)(2,1)S(1)} %reshape.6.x_hbm, s32[1,1,256]{2,1,0:T(1,128)S(1)} %copy-done.2, bf16[1,8,3072]{2,1,0:T(8,128)(2,1)S(1)} %copy-done.1, bf16[1,768,3072]{2,1,0:T(8,128)(2,1)S(1)} %copy-done), custom_call_target="tpu_custom_call" | custom-call | flops 553648128 | bytes 7864320 | tf_op jit(solution)/shard_map/pallas_call | solution.py:337
  33.5 0.9 %copy.6 = bf16[1,1,128,3072]{3,2,1,0:T(8,128)(2,1)} copy(bf16[1,1,128,3072]{3,2,1,0:T(8,128)(2,1)S(1)} %bitcast.3) | data formatting | bytes 1572864
Async XLA Ops:
  0.0 3.0 %copy-start.1 = (bf16[1,8,3072]{2,1,0:T(8,128)(2,1)S(1)}, bf16[1,8,3072]{2,1,0:T(8,128)(2,1)}, u32[]{:S(2)}) copy-start(bf16[1,8,3072]{2,1,0:T(8,128)(2,1)} %cond_ref.1) | copy-start | bytes 147460
  0.0 3.0 %copy-start.2 = (s32[1,1,256]{2,1,0:T(1,128)S(1)}, s32[1,1,256]{2,1,0:T(1,128)}, u32[]{:S(2)}) copy-start(s32[1,1,256]{2,1,0:T(1,128)} %seg_ref.1) | copy-start | bytes 3076
  3.0 2.3 %copy-start = (bf16[1,768,3072]{2,1,0:T(8,128)(2,1)S(1)}, bf16[1,768,3072]{2,1,0:T(8,128)(2,1)}, u32[]{:S(2)}) copy-start(bf16[1,768,3072]{2,1,0:T(8,128)(2,1)} %w_hbm.1) | copy-start | bytes 14155780

commit v3 on v2

--- a/solution.py
+++ b/solution.py
@@ -365,7 +365,7 @@
             dma((chunks,)),
         ],
         compiler_params=pltpu.CompilerParams(
-            collective_id=0, has_side_effects=True, vmem_limit_bytes=40 * 1024 * 1024
+            collective_id=0, has_side_effects=True, vmem_limit_bytes=49 * 1024 * 1024
         ),
         cost_estimate=pl.CostEstimate(
             flops=4 * tok * keys * width + 2 * n_dp * samples * w_rows * width,

time: 34.6 us -> 31.9 us (0.922)
  local copies, waits for them, and re-layouts: 6.18 us -> 3.85 us
    unnamed x7 -> x5, local copies, waits for them, and re-layouts: 3.22 us -> 0.89 us
where the time goes in v3:
time: 31.9 us; the launch traced here: 31.8 us
  Pallas kernels  27.9 us (87%)
  local copies, waits for them, and re-layouts  3.85 us (12%)
    pallas_call x1, Pallas kernels, shards(): pl.pallas_call(functools.partial(relay_kernel, sizes), out_shape=jax.Shap...  27.9 us
    reshape x1, local copies, waits for them, and re-layouts, shards(): projected.reshape(tok, 3 * width)  2.96 us
    unnamed x5, local copies, waits for them, and re-layouts  0.89 us

profile of v3, /device:TPU:0, one launch (start us, length us, event | category | flops | bytes accessed | tf_op | source)
XLA Modules:
  0.0 31.8 jit_solution(4425823802712815576)
XLA Ops:
  0.0 0.0 copy-start
  0.0 0.0 copy-start.1
  0.0 3.0 %reshape.6.x_hbm = bf16[128,9216]{1,0:T(8,128)(2,1)S(1)} reshape(bf16[1,1,128,3,24,128]{5,4,3,2,1,0:T(8,128)(2,1)} %param.4) | data formatting | bytes 4718592 | tf_op jit(solution)/shard_map/reshape | solution.py:375
  3.0 0.0 copy-done
  3.0 0.0 copy-done.1
  3.0 27.9 %shard_map.46 = bf16[128,3072]{1,0:T(8,128)(2,1)S(1)} custom-call(bf16[128,9216]{1,0:T(8,128)(2,1)S(1)} %reshape.6.x_hbm, s32[1,1,256]{2,1,0:T(1,128)S(1)} %copy-done.1, bf16[1,8,3072]{2,1,0:T(8,128)(2,1)S(1)} %copy-done, bf16[1,768,3072]{2,1,0:T(8,128)(2,1)} %w_hbm.1), custom_call_target="tpu_custom_call" | custom-call | flops 553648128 | bytes 7864320 | tf_op jit(solution)/shard_map/pallas_call | solution.py:337
  30.9 0.9 %copy.6 = bf16[1,1,128,3072]{3,2,1,0:T(8,128)(2,1)} copy(bf16[1,1,128,3072]{3,2,1,0:T(8,128)(2,1)S(1)} %bitcast.3) | data formatting | bytes 1572864
Async XLA Ops:
  0.0 3.0 %copy-start = (bf16[1,8,3072]{2,1,0:T(8,128)(2,1)S(1)}, bf16[1,8,3072]{2,1,0:T(8,128)(2,1)}, u32[]{:S(2)}) copy-start(bf16[1,8,3072]{2,1,0:T(8,128)(2,1)} %cond_ref.1) | copy-start | bytes 147460
  0.0 3.0 %copy-start.1 = (s32[1,1,256]{2,1,0:T(1,128)S(1)}, s32[1,1,256]{2,1,0:T(1,128)}, u32[]{:S(2)}) copy-start(s32[1,1,256]{2,1,0:T(1,128)} %seg_ref.1) | copy-start | bytes 3076

commit v4 on v3

--- a/solution.py
+++ b/solution.py
@@ -17,12 +17,11 @@
 
 def relay_kernel(
     sizes,
-    x_hbm,
+    x_ref,
     seg_ref,
     cond_ref,
     w_hbm,
     out_hbm,
-    x_vmem,
     w_vmem,
     k_halo,
     v_halo,
@@ -33,7 +32,6 @@
     gate_parts,
     gate_split,
     bias,
-    x_sem,
     w_sem,
     k_send,
     k_recv,
@@ -66,9 +64,7 @@
         exchanges = [(right, tok - reach, left, tok - reach), (left, 0, right, 0)]
     slots = len(exchanges)
 
-    x_copy = pltpu.make_async_copy(x_hbm, x_vmem, x_sem)
     w_copy = pltpu.make_async_copy(w_hbm.at[0], w_vmem, w_sem)
-    x_copy.start()
     w_copy.start()
 
     barrier = pltpu.get_barrier_semaphore()
@@ -111,7 +107,7 @@
         for part, held, send, recv in ((1, k_halo, k_send, k_recv), (2, v_halo, v_send, v_recv)):
             result.append(
                 pltpu.make_async_remote_copy(
-                    src_ref=x_hbm.at[rows, pl.ds(part * width + lanes, chunk)],
+                    src_ref=x_ref.at[rows, pl.ds(part * width + lanes, chunk)],
                     dst_ref=held.at[slot, rows, pl.ds(lanes, chunk)],
                     send_sem=send.at[slot, c],
                     recv_sem=recv.at[slot, c],
@@ -129,7 +125,7 @@
         for part, held, send, recv in ((1, k_halo, k_send, k_recv), (2, v_halo, v_send, v_recv)):
             result.append(
                 pltpu.make_async_remote_copy(
-                    src_ref=x_hbm.at[rows, pl.ds(part * width + lanes, chunk)],
+                    src_ref=x_ref.at[rows, pl.ds(part * width + lanes, chunk)],
                     dst_ref=held.at[slot, rows, pl.ds(lanes, chunk)],
                     send_sem=send.at[slot, c],
                     recv_sem=recv.at[slot, c],
@@ -227,7 +223,6 @@
 
     lax.fori_loop(0, tiles, gate_tile, 0)
 
-    x_copy.wait()
     factor = math.log2(math.e) / math.sqrt(size)
     contract_last = (((1,), (1,)), ((), ()))
 
@@ -239,9 +234,9 @@
         for h in range(HEADS_PER_CHUNK):
             lane = base + h * size
             lanes = pl.ds(lane, size)
-            query = x_vmem[:, lanes]
-            keys = [x_vmem[:, pl.ds(width + lane, size)]]
-            values = [x_vmem[:, pl.ds(2 * width + lane, size)]]
+            query = x_ref[:, lanes]
+            keys = [x_ref[:, pl.ds(width + lane, size)]]
+            values = [x_ref[:, pl.ds(2 * width + lane, size)]]
             for slot in range(slots):
                 keys.append(k_halo[slot, :, lanes])
                 values.append(v_halo[slot, :, lanes])
@@ -337,10 +332,9 @@
     handed = pl.pallas_call(
         functools.partial(relay_kernel, sizes),
         out_shape=jax.ShapeDtypeStruct((tok, width), jnp.bfloat16),
-        in_specs=[anywhere, inside, inside, pl.BlockSpec(memory_space=pltpu.HBM)],
+        in_specs=[inside, inside, inside, pl.BlockSpec(memory_space=pltpu.HBM)],
         out_specs=anywhere,
         scratch_shapes=[
-            pltpu.VMEM((tok, 3 * width), jnp.bfloat16),
             pltpu.VMEM((w_rows, width), jnp.bfloat16),
             pltpu.VMEM((max(slots, 1), tok, width), jnp.bfloat16),
             pltpu.VMEM((max(slots, 1), tok, width), jnp.bfloat16),
@@ -351,7 +345,6 @@
             pltpu.VMEM((n_dp, samples, width), jnp.float32),
             pltpu.VMEM((2 * samples, width), jnp.bfloat16),
             pltpu.VMEM((tok, keys), jnp.float32),
-            dma,
             dma,
             dma((max(slots, 1), chunks)),
             dma((max(slots, 1), chunks)),

time: 31.9 us -> 31.7 us (level)
  no operation moved by 1% of the time
where the time goes in v4:
time: 31.7 us; the launch traced here: 31.6 us
  Pallas kernels  27.7 us (87%)
  local copies, waits for them, and re-layouts  3.85 us (12%)
    pallas_call x1, Pallas kernels, shards(): pl.pallas_call(functools.partial(relay_kernel, sizes), out_shape=jax.Shap...  27.7 us
    reshape x1, local copies, waits for them, and re-layouts, shards(): projected.reshape(tok, 3 * width)  2.96 us
    unnamed x5, local copies, waits for them, and re-layouts  0.89 us

profile of v4, /device:TPU:0, one launch (start us, length us, event | category | flops | bytes accessed | tf_op | source)
XLA Modules:
  0.0 31.6 jit_solution(13676246590941399800)
XLA Ops:
  0.0 0.0 copy-start
  0.0 0.0 copy-start.1
  0.0 3.0 %reshape.6.x_ref = bf16[128,9216]{1,0:T(8,128)(2,1)S(1)} reshape(bf16[1,1,128,3,24,128]{5,4,3,2,1,0:T(8,128)(2,1)} %param.4) | data formatting | bytes 4718592 | tf_op jit(solution)/shard_map/reshape | solution.py:368
  3.0 0.0 copy-done
  3.0 0.0 copy-done.1
  3.0 27.7 %shard_map.46 = bf16[128,3072]{1,0:T(8,128)(2,1)S(1)} custom-call(bf16[128,9216]{1,0:T(8,128)(2,1)S(1)} %reshape.6.x_ref, s32[1,1,256]{2,1,0:T(1,128)S(1)} %copy-done.1, bf16[1,8,3072]{2,1,0:T(8,128)(2,1)S(1)} %copy-done, bf16[1,768,3072]{2,1,0:T(8,128)(2,1)} %w_hbm.1), custom_call_target="tpu_custom_call" | custom-call | flops 553648128 | bytes 7864320 | tf_op jit(solution)/shard_map/pallas_call | solution.py:332
  30.7 0.9 %copy.6 = bf16[1,1,128,3072]{3,2,1,0:T(8,128)(2,1)} copy(bf16[1,1,128,3072]{3,2,1,0:T(8,128)(2,1)S(1)} %bitcast.3) | data formatting | bytes 1572864
Async XLA Ops:
  0.0 3.0 %copy-start = (bf16[1,8,3072]{2,1,0:T(8,128)(2,1)S(1)}, bf16[1,8,3072]{2,1,0:T(8,128)(2,1)}, u32[]{:S(2)}) copy-start(bf16[1,8,3072]{2,1,0:T(8,128)(2,1)} %cond_ref.1) | copy-start | bytes 147460
  0.0 3.0 %copy-start.1 = (s32[1,1,256]{2,1,0:T(1,128)S(1)}, s32[1,1,256]{2,1,0:T(1,128)}, u32[]{:S(2)}) copy-start(s32[1,1,256]{2,1,0:T(1,128)} %seg_ref.1) | copy-start | bytes 3076

commit v5 on v4

--- a/solution.py
+++ b/solution.py
@@ -162,15 +162,15 @@
         act_copy(d).start()
         return carry
 
-    lax.fori_loop(1, n_dp, start_act, 0)
-
     def start_halo(c, carry):
         for slot in range(slots):
             for copy in halo_copies(slot, c):
                 copy.start()
         return carry
 
-    lax.fori_loop(0, chunks, start_halo, 0)
+    lax.fori_loop(0, 1, start_halo, 0)
+    lax.fori_loop(1, n_dp, start_act, 0)
+    lax.fori_loop(1, chunks, start_halo, 0)
 
     if slots and reach < tok:
         for slot in range(slots):

time: 31.7 us -> 31.7 us (level)
  no operation moved by 1% of the time
where the time goes in v5:
time: 31.7 us; the launch traced here: 31.6 us
  Pallas kernels  27.7 us (87%)
  local copies, waits for them, and re-layouts  3.85 us (12%)
    pallas_call x1, Pallas kernels, shards(): pl.pallas_call(functools.partial(relay_kernel, sizes), out_shape=jax.Shap...  27.7 us
    reshape x1, local copies, waits for them, and re-layouts, shards(): projected.reshape(tok, 3 * width)  2.96 us
    unnamed x5, local copies, waits for them, and re-layouts  0.89 us

profile of v5, /device:TPU:0, one launch (start us, length us, event | category | flops | bytes accessed | tf_op | source)
XLA Modules:
  0.0 31.6 jit_solution(7822639461355703803)
XLA Ops:
  0.0 0.0 copy-start
  0.0 0.0 copy-start.1
  0.0 3.0 %reshape.6.x_ref = bf16[128,9216]{1,0:T(8,128)(2,1)S(1)} reshape(bf16[1,1,128,3,24,128]{5,4,3,2,1,0:T(8,128)(2,1)} %param.4) | data formatting | bytes 4718592 | tf_op jit(solution)/shard_map/reshape | solution.py:368
  3.0 0.0 copy-done
  3.0 0.0 copy-done.1
  3.0 27.7 %shard_map.46 = bf16[128,3072]{1,0:T(8,128)(2,1)S(1)} custom-call(bf16[128,9216]{1,0:T(8,128)(2,1)S(1)} %reshape.6.x_ref, s32[1,1,256]{2,1,0:T(1,128)S(1)} %copy-done.1, bf16[1,8,3072]{2,1,0:T(8,128)(2,1)S(1)} %copy-done, bf16[1,768,3072]{2,1,0:T(8,128)(2,1)} %w_hbm.1), custom_call_target="tpu_custom_call" | custom-call | flops 553648128 | bytes 7864320 | tf_op jit(solution)/shard_map/pallas_call | solution.py:332
  30.7 0.9 %copy.6 = bf16[1,1,128,3072]{3,2,1,0:T(8,128)(2,1)} copy(bf16[1,1,128,3072]{3,2,1,0:T(8,128)(2,1)S(1)} %bitcast.3) | data formatting | bytes 1572864
Async XLA Ops:
  0.0 3.0 %copy-start = (bf16[1,8,3072]{2,1,0:T(8,128)(2,1)S(1)}, bf16[1,8,3072]{2,1,0:T(8,128)(2,1)}, u32[]{:S(2)}) copy-start(bf16[1,8,3072]{2,1,0:T(8,128)(2,1)} %cond_ref.1) | copy-start | bytes 147460
  0.0 3.0 %copy-start.1 = (s32[1,1,256]{2,1,0:T(1,128)S(1)}, s32[1,1,256]{2,1,0:T(1,128)}, u32[]{:S(2)}) copy-start(s32[1,1,256]{2,1,0:T(1,128)} %seg_ref.1) | copy-start | bytes 3076
